TPU v7x, 32 devices: a whole 2x2x4 slice. The times are simulated.
32 devices in a mesh: graphs: 8 (over z, y), leaves: 4 (over x, core).
Axes of the slice: x: 2, y: 2, z: 4, core: 2. Of those that a mesh axis runs over, the one named last changes fastest.
Arguments:
- centers: float32 [1024, 300], P('graphs'), may hold values from -6 to 6
- leaf_nodes: float32 [1024, 16, 300], P('graphs', 'leaves'), may hold values from -6 to 6
- edges: float32 [1024, 16, 300], P('graphs', 'leaves'), may hold values from -6 to 6
- leaf_counts: int32 [1024], P('graphs'), may hold values from 1 to 16, as said below
- square: float32 [2, 4, 300, 300], replicated, may hold values from -0.375 to 0.375
- out_proj: float32 [2, 300, 300], replicated, may hold values from -1 to 1
- ff_in: float32 [2, 300, 1200], replicated, may hold values from -0.375 to 0.375
- ff_out: float32 [2, 1200, 300], replicated, may hold values from -0.1875 to 0.1875
- ff_bias: float32 [2, 1200], replicated, may hold values from -2 to 2
- biases: float32 [2, 7, 300], replicated, may hold values from -2 to 2
- gains: float32 [2, 2, 300], replicated, may hold values from 0.5 to 1.5
- cot_center: float32 [1024, 300], P('graphs'), may hold values from -6 to 6
- cot_edges: float32 [1024, 16, 300], P('graphs', 'leaves'), may hold values from -6 to 6
Outputs:
- center_out: float32 [1024, 300], P('graphs')
- edges_out: float32 [1024, 16, 300], P('graphs', 'leaves')
- grad_center: float32 [1024, 300], P('graphs')
- grad_leaf_nodes: float32 [1024, 16, 300], P('graphs', 'leaves')
- grad_edges: float32 [1024, 16, 300], P('graphs', 'leaves')
- grad_square: float32 [2, 4, 300, 300], replicated
- grad_out_proj: float32 [2, 300, 300], replicated
- grad_ff_in: float32 [2, 300, 1200], replicated
- grad_ff_out: float32 [2, 1200, 300], replicated
- grad_ff_bias: float32 [2, 1200], replicated
- grad_biases: float32 [2, 7, 300], replicated
- grad_gains: float32 [2, 2, 300], replicated
Inputs may be any that keep to these rules, and one draw needn't show every extreme that they name: `leaf_counts`: in every aligned block of 128 graphs one graph has all 16 leaves live.
All inputs are finite; a program needn't handle non-finite values.
Results may differ from a plain program's by a relative error of at most 0.0003.
Values sent between devices are 32-bit elements; how exact they have to be, the bound alone decides.
No kernel may reach another device: no remote copies, remote signals or barrier semaphores. Data moves between devices by JAX's collectives and lax.ppermute only.
A program may use at most 192 MiB of HBM per device.

v0:
```python
import jax
import jax.numpy as jnp
from jax import lax
from jax.sharding import PartitionSpec as P

HEADS = 12
HEAD_DIM = 25
LAYERS = 2


precise = lax.Precision.HIGHEST


def matmul_hi(left, right):
    return jnp.dot(left, right, precision=precise)


def layer_norm(values, gain, shift):
    centred = values - jnp.mean(values, axis=-1, keepdims=True)
    spread = jnp.mean(centred * centred, axis=-1, keepdims=True)
    return centred * lax.rsqrt(spread + 1e-05) * gain + shift


def center_block(
    attended, states, out_weight, in_weight, down_weight, hidden_bias, center_bias, norm_gains
):
    projected = matmul_hi(attended, out_weight) + center_bias[1]
    normed_one = layer_norm(states + projected, norm_gains[0], center_bias[2])
    hidden_act = jax.nn.gelu(matmul_hi(normed_one, in_weight) + hidden_bias, approximate=True)
    ff_result = matmul_hi(hidden_act, down_weight) + center_bias[3]
    return layer_norm(normed_one + ff_result, norm_gains[1], center_bias[4])


def split_heads(rows):
    return rows.reshape(rows.shape[:-1] + (HEADS, HEAD_DIM))


def on_device(
    centers,
    leaf_nodes,
    edges,
    leaf_counts,
    square,
    out_proj,
    ff_in,
    ff_out,
    ff_bias,
    biases,
    gains,
    cot_center,
    cot_edges,
):
    graph_count, slot_count, width = leaf_nodes.shape
    row_count = graph_count * slot_count
    slot_index = lax.axis_index("leaves") * slot_count + jnp.arange(slot_count, dtype=jnp.int32)
    live_mask = slot_index[None, :] < leaf_counts[:, None]
    head_mask = live_mask[:, None, :]
    scale = HEAD_DIM ** (-0.5)

    def project(states, edge_rows, layer_at):
        messages = (leaf_nodes * edge_rows).reshape(row_count, width)
        queries = matmul_hi(states, square[layer_at, 0]) + biases[layer_at, 0]
        key_rows = matmul_hi(messages, square[layer_at, 1]).reshape(
            graph_count, slot_count, HEADS, HEAD_DIM
        )
        value_rows = (matmul_hi(messages, square[layer_at, 2]) + biases[layer_at, 5]).reshape(
            graph_count, slot_count, HEADS, HEAD_DIM
        )
        scores = (
            jnp.einsum("ghc,gshc->ghs", split_heads(queries), key_rows, precision=precise) * scale
        )
        scores = jnp.where(head_mask, scores, -1e30)
        return (messages, queries, key_rows, value_rows, scores)

    states, edge_rows = (centers, edges)
    kept = []
    for layer_at in range(LAYERS):
        messages, queries, key_rows, value_rows, scores = project(states, edge_rows, layer_at)
        local_top = jnp.max(scores, axis=-1)
        weights = jnp.where(head_mask, jnp.exp(scores - local_top[..., None]), 0.0)
        local_total = jnp.sum(weights, axis=-1)
        local_sum = jnp.einsum("ghs,gshc->ghc", weights, value_rows, precision=precise).reshape(
            graph_count, width
        )
        top_score = lax.pmax(local_top, "leaves")
        factor = jnp.exp(local_top - top_score)
        summed, totals = lax.psum(
            (local_sum * jnp.repeat(factor, HEAD_DIM, axis=-1), local_total * factor), "leaves"
        )
        attended = (split_heads(summed) / totals[..., None]).reshape(graph_count, width)
        kept.append((states, edge_rows, top_score, totals, attended))
        next_states = center_block(
            attended,
            states,
            out_proj[layer_at],
            ff_in[layer_at],
            ff_out[layer_at],
            ff_bias[layer_at],
            biases[layer_at, 0:5],
            gains[layer_at],
        )
        edge_rows = edge_rows + (
            matmul_hi(messages, square[layer_at, 3]) + biases[layer_at, 6]
        ).reshape(graph_count, slot_count, width)
        states = next_states
    center_out, edges_out = (states, edge_rows)
    grad_states, grad_edge = (cot_center, cot_edges)
    grad_nodes = jnp.zeros_like(leaf_nodes)
    center_parts = [None] * LAYERS
    leaf_parts = [None] * LAYERS
    for layer_at in reversed(range(LAYERS)):
        states, edge_rows, top_score, totals, attended = kept[layer_at]
        messages, queries, key_rows, value_rows, scores = project(states, edge_rows, layer_at)
        probs = (
            jnp.where(head_mask, jnp.exp(scores - top_score[..., None]), 0.0) / totals[..., None]
        )
        unused_out, pullback = jax.vjp(
            center_block,
            attended,
            states,
            out_proj[layer_at],
            ff_in[layer_at],
            ff_out[layer_at],
            ff_bias[layer_at],
            biases[layer_at, 0:5],
            gains[layer_at],
        )
        grad_att, grad_res, grad_outw, grad_inw, grad_downw, grad_hidden, grad_cbias, grad_gain = (
            pullback(grad_states)
        )
        att_heads = split_heads(grad_att)
        grad_values = jnp.einsum("ghs,ghc->gshc", probs, att_heads, precision=precise).reshape(
            row_count, width
        )
        grad_probs = jnp.einsum("ghc,gshc->ghs", att_heads, value_rows, precision=precise)
        centre_term = jnp.sum(att_heads * split_heads(attended), axis=-1)
        grad_scores = probs * (grad_probs - centre_term[..., None]) * scale
        query_part = jnp.einsum("ghs,gshc->ghc", grad_scores, key_rows, precision=precise).reshape(
            graph_count, width
        )
        grad_keys = jnp.einsum(
            "ghs,ghc->gshc", grad_scores, split_heads(queries), precision=precise
        ).reshape(row_count, width)
        grad_queries = lax.psum(query_part, "leaves")
        edge_flat = grad_edge.reshape(row_count, width)
        grad_messages = (
            matmul_hi(grad_keys, square[layer_at, 1].T)
            + matmul_hi(grad_values, square[layer_at, 2].T)
            + matmul_hi(edge_flat, square[layer_at, 3].T)
        )
        grad_messages = grad_messages.reshape(graph_count, slot_count, width)
        leaf_square = jnp.stack(
            [
                matmul_hi(messages.T, grad_keys),
                matmul_hi(messages.T, grad_values),
                matmul_hi(messages.T, edge_flat),
            ]
        )
        leaf_bias = jnp.stack([jnp.sum(grad_values, axis=0), jnp.sum(edge_flat, axis=0)])
        grad_nodes = grad_nodes + grad_messages * edge_rows
        grad_edge = grad_edge + grad_messages * leaf_nodes
        query_square = matmul_hi(states.T, grad_queries)[None]
        center_bias = jnp.concatenate([jnp.sum(grad_queries, axis=0)[None], grad_cbias[1:]], axis=0)
        grad_states = grad_res + matmul_hi(grad_queries, square[layer_at, 0].T)
        center_parts[layer_at] = (
            query_square,
            grad_outw,
            grad_inw,
            grad_downw,
            grad_hidden,
            grad_gain,
            center_bias,
        )
        leaf_parts[layer_at] = (leaf_square, leaf_bias)
    center_stack = [
        jnp.stack([center_parts[layer_at][member] for layer_at in range(LAYERS)])
        for member in range(7)
    ]
    leaf_stack = [
        jnp.stack([leaf_parts[layer_at][member] for layer_at in range(LAYERS)])
        for member in range(2)
    ]
    center_sum = lax.psum(
        (
            center_stack[0],
            center_stack[1],
            center_stack[2],
            center_stack[3],
            center_stack[4],
            center_stack[5],
            center_stack[6],
        ),
        "graphs",
    )
    leaf_sum = lax.psum((leaf_stack[0], leaf_stack[1]), ("graphs", "leaves"))
    grad_square = jnp.concatenate([center_sum[0], leaf_sum[0]], axis=1)
    grad_biases = jnp.concatenate([center_sum[6], leaf_sum[1]], axis=1)
    return (
        center_out,
        edges_out,
        grad_states,
        grad_nodes,
        grad_edge,
        grad_square,
        center_sum[1],
        center_sum[2],
        center_sum[3],
        center_sum[4],
        grad_biases,
        center_sum[5],
    )


def solution(mesh):
    in_specs = (
        P("graphs", None),
        P("graphs", "leaves", None),
        P("graphs", "leaves", None),
        P("graphs"),
        P(),
        P(),
        P(),
        P(),
        P(),
        P(),
        P(),
        P("graphs", None),
        P("graphs", "leaves", None),
    )
    out_specs = (
        P("graphs", None),
        P("graphs", "leaves", None),
        P("graphs", None),
        P("graphs", "leaves", None),
        P("graphs", "leaves", None),
        P(),
        P(),
        P(),
        P(),
        P(),
        P(),
        P(),
    )
    return jax.shard_map(
        on_device, mesh=mesh, in_specs=in_specs, out_specs=out_specs, check_vma=False
    )
```

profile of v0, /device:TPU:0, one launch (start us, length us, event | category | flops | bytes accessed | tf_op | source)
XLA Modules:
  0.0 726.5 jit_solution(16775836248284346889)
XLA Ops:
  8.8 10.2 %fusion.118 = (f32[1,1,300,300]{3,1,2,0:T(1,128)}, f32[1,1,300,300]{3,1,2,0:T(1,128)}, f32[1,1,300,300]{3,1,2,0:T(1,128)}, f32[1,1,300,300]{3,1,2,0:T(1,128)}, f...) fusion(f32[2,4,300,300]{3,1,2,0:T(4,128)} %param.17), kind=kLoop, calls=%fused_computation.282 | loop fusion | bytes 5760000 | tf_op jit(solution)/shard_map/slice | solution.py:103
  27.2 13.4 %pmax.14 = f32[128,12]{1,0:T(8,128)S(1)} all-reduce(f32[128,12]{1,0:T(8,128)S(1)} %fusion.44), channel_id=1, replica_groups=mesh['graphs'=8,'leaves'=4] {'leaves'}, use_global_device_ids=true, to_apply=%region_1.2 | all-reduce | flops 1536 | bytes 12288 | tf_op jit(solution)/shard_map/pmax | solution.py:85
  52.5 12.0 %psum.106 = f32[128,12]{1,0:T(8,128)S(1)} all-reduce(f32[128,12]{1,0:T(8,128)} %get-tuple-element.105), channel_id=1, replica_groups=mesh['graphs'=8,'leaves'=4] {'leaves'}, use_global_device_ids=true, to_apply=%region_4.5 | all-reduce | flops 1536 | bytes 12288 | tf_op jit(solution)/shard_map/psum | solution.py:87
  66.9 6.7 fusion.119
  97.5 4.6 reshape.359
  118.2 10.7 %pmax.15 = f32[128,12]{1,0:T(8,128)S(1)} all-reduce(f32[128,12]{1,0:T(8,128)S(1)} %fusion.45), channel_id=1, replica_groups=mesh['graphs'=8,'leaves'=4] {'leaves'}, use_global_device_ids=true, to_apply=%region_10.11 | all-reduce | flops 1536 | bytes 12288 | tf_op jit(solution)/shard_map/pmax | solution.py:85
  136.7 13.0 %psum.108 = f32[128,12]{1,0:T(8,128)} all-reduce(f32[128,12]{1,0:T(8,128)} %get-tuple-element.101), channel_id=1, replica_groups=mesh['graphs'=8,'leaves'=4] {'leaves'}, use_global_device_ids=true, to_apply=%region_13.14 | all-reduce | flops 1536 | bytes 12288 | tf_op jit(solution)/shard_map/psum | solution.py:87
  154.5 11.3 %all-reduce.23.cloned.1.call-done = f32[128,300]{0,1:T(8,128)} async-done(((f32[128,300]{0,1:T(8,128)}), f32[128,300]{0,1:T(8,128)}) %all-reduce.23.cloned.1.call-update) | async-done | bytes 153616 | tf_op jit(solution)/shard_map/psum | solution.py:87
  176.0 4.2 fusion.126
  189.5 4.2 multiply_reduce_fusion.1
  202.9 29.4 %all-reduce.25.cloned.1.call-done = f32[128,300]{0,1:T(8,128)} async-done(((f32[128,300]{0,1:T(8,128)}), f32[128,300]{0,1:T(8,128)}) %all-reduce.25.cloned.1.call-update) | async-done | bytes 153616 | tf_op jit(solution)/shard_map/psum | solution.py:144
  234.3 4.7 fusion.127
  249.5 4.6 multiply_reduce_fusion
  266.6 24.1 %all-reduce.27.cloned.1.call-done = f32[128,300]{0,1:T(8,128)} async-done(((f32[128,300]{0,1:T(8,128)}), f32[128,300]{0,1:T(8,128)}) %all-reduce.27.cloned.1.call-update) | async-done | bytes 153616 | tf_op jit(solution)/shard_map/psum | solution.py:144
  308.0 4.5 convolution_bitcast_fusion.6
  314.7 7.3 %multiply_bitcast_fusion.2 = (f32[128,4,12,25]{3,2,1,0:T(8,128)}, f32[128,4,12,25]{3,2,1,0:T(8,128)}) fusion(f32[128,12,25]{2,1,0:T(8,128)S(1)} %copy.244, f32[128,12,4]{1,2,0:T(4,128)} %get-tuple-element.96, f32[128,12,4]{1,2,0:T(4,128)} %get-tuple-element.95, f32[128,12,25]{2,1,0:T(8,128)} %copy.142), kind=kLoop, calls=%fused_computation.6 | loop fusion | flops 307200 | bytes 1585152 | tf_op jit(solution)/shard_map/ghs,ghc->gshc/transpose | solution.py:132
  325.6 4.5 reshape.366
  355.5 7.1 multiply_bitcast_fusion
  398.1 40.8 %psum.118 = f32[2,2,300]{2,1,0:T(2,128)S(1)} all-reduce(f32[2,2,300]{2,1,0:T(2,128)S(1)} %pad_maximum_fusion.9), channel_id=1, replica_groups=mesh['graphs'=8,'leaves'=4] {'graphs','leaves'}, use_global_device_ids=true, to_apply=%region_53.54 | all-reduce | flops 1200 | bytes 9600 | tf_op jit(solution)/shard_map/psum | solution.py:195
  439.1 38.6 %all-reduce.12 = (f32[2,1200]{1,0:T(2,128)}, f32[2,5,300]{2,1,0:T(8,128)S(1)}, f32[2,2,300]{2,1,0:T(2,128)}) all-reduce(f32[2,1200]{1,0:T(2,128)S(1)} %pad_maximum_fusion.8, f32[2,5,300]{2,1,0:T(8,128)S(1)} %pad_maximum_fusion.6, f32[2,2,300]{2,1,0:T(2,128)S(1)} %pad_maximum_fusion.10), channel_id=1, replica_groups=mesh['graphs'=8,'leaves'=4] {'graphs'}, use_global_device_ids=true, to_apply=%region_37.38 | all-reduce | flops 6600 | bytes 52800 | tf_op jit(solution)/shard_map/psum | solution.py:183
  479.5 83.9 %all-reduce.31.cloned.1.call-done = (f32[2,1,300,300]{2,3,1,0:T(8,128)}, f32[2,300,300]{2,1,0:T(8,128)}, f32[2,300,1200]{2,1,0:T(8,128)}, f32[2,1200,300]{1,2,0:T(8,128)}) async-done(((f32[2,1,300,300]{2,3,1,0:T(8,128)}, f32[2,300,300]{2,1,0:T(8,128)}, f32[2,300,1200]{2,1,0:T(8,128)}, f32[2,1200,300]{1,2,0:T(8,128)}), (f32[2,1,300,300]{2,3,1,0:T(8,128)}, f32[2,300,300]{2,1,0:T(8,128)}, ...) | async-done | bytes 7200016 | tf_op jit(solution)/shard_map/psum | solution.py:183
  564.9 139.8 %all-reduce.29.cloned.1.call-done = f32[2,3,300,300]{3,2,1,0:T(8,128)} async-done(((f32[2,3,300,300]{3,2,1,0:T(8,128)}), f32[2,3,300,300]{3,2,1,0:T(8,128)}) %all-reduce.29.cloned.1.call-update) | async-done | bytes 2160016 | tf_op jit(solution)/shard_map/psum | solution.py:195
  710.1 4.0 copy.164
  714.1 4.0 copy.165
  (453 shorter events, 222.8 us)
Async XLA Ops:
  7.2 95.7 %all-reduce.21.cloned.1.call-start = ((), (), s32[]{:S(2)}) async-start(), calls=%async_computation | async-start | bytes 311296 | tf_op jit(solution)/shard_map/psum | solution.py:87
  8.7 100.9 %copy-start.84 = (f32[300]{0:T(512)}, f32[300]{0:T(512)S(1)}, u32[]{:S(2)}) copy-start(f32[300]{0:T(512)S(1)} %get-tuple-element.69) | copy-start | bytes 3604
  18.9 23.0 %copy-start.26 = (f32[1,1,300,300]{3,1,2,0:T(1,128)}, f32[1,1,300,300]{3,1,2,0:T(1,128)S(1)}, u32[]{:S(2)}) copy-start(f32[1,1,300,300]{3,1,2,0:T(1,128)S(1)} %get-tuple-element.116) | copy-start | bytes 1080004
  23.1 17.5 %copy-start.8 = (f32[128,4,300]{0,1,2:T(4,128)}, f32[128,4,300]{0,1,2:T(4,128)S(1)}, u32[]{:S(2)}) copy-start(f32[128,4,300]{0,1,2:T(4,128)S(1)} %mul.404) | copy-start | bytes 1843204
  25.7 16.3 %copy-start.34 = (f32[128,12,4]{1,2,0:T(4,128)}, f32[128,12,4]{1,2,0:T(4,128)S(1)}, u32[]{:S(2)}) copy-start(f32[128,12,4]{1,2,0:T(4,128)S(1)} %copy.174) | copy-start | bytes 73732
  50.9 114.9 %all-reduce.23.cloned.1.call-start = ((), (), s32[]{:S(2)}) async-start(), calls=%async_computation.1 | async-start | bytes 311296 | tf_op jit(solution)/shard_map/psum | solution.py:87
  51.3 36.8 %copy-start.6 = (f32[128,4,300]{2,1,0:T(4,128)}, f32[128,4,300]{2,1,0:T(4,128)S(1)}, u32[]{:S(2)}) copy-start(f32[128,4,300]{2,1,0:T(4,128)S(1)} %copy.127) | copy-start | bytes 1843204
  51.3 13.8 %copy-start.75 = (f32[2,300,300]{2,0,1:T(2,128)S(1)}, f32[2,300,300]{2,0,1:T(2,128)}, u32[]{:S(2)}) copy-start(f32[2,300,300]{2,0,1:T(2,128)} %param.18) | copy-start | bytes 2160004
  73.6 32.6 %copy-start.1 = (f32[1,300,1200]{2,0,1:T(1,128)}, f32[1,300,1200]{2,0,1:T(1,128)S(1)}, u32[]{:S(2)}) copy-start(f32[1,300,1200]{2,0,1:T(1,128)S(1)} %get-tuple-element.119) | copy-start | bytes 4320004
  111.3 55.5 %copy-start.86 = (f32[128]{0:T(128)}, f32[128]{0:T(128)S(1)}, u32[]{:S(2)}) copy-start(f32[128]{0:T(128)S(1)} %broadcast_multiply_fusion.4) | copy-start | bytes 1540
  116.9 15.8 %copy-start.36 = (f32[128,12,4]{1,2,0:T(4,128)}, f32[128,12,4]{1,2,0:T(4,128)S(1)}, u32[]{:S(2)}) copy-start(f32[128,12,4]{1,2,0:T(4,128)S(1)} %copy.189) | copy-start | bytes 73732
  133.8 98.5 %all-reduce.25.cloned.1.call-start = ((), (), s32[]{:S(2)}) async-start(), calls=%async_computation.2 | async-start | bytes 311296 | tf_op jit(solution)/shard_map/psum | solution.py:144
  136.7 32.5 %copy-start.3 = (f32[1,300,1200]{2,0,1:T(1,128)S(1)}, f32[1,300,1200]{2,0,1:T(1,128)}, u32[]{:S(2)}) copy-start(f32[1,300,1200]{2,0,1:T(1,128)} %get-tuple-element.120) | copy-start | bytes 4320004
  188.2 44.0 %copy-start.104 = (f32[128]{0:T(128)}, f32[128]{0:T(128)S(1)}, u32[]{:S(2)}) copy-start(f32[128]{0:T(128)S(1)} %negate_multiply_fusion.2) | copy-start | bytes 1540
  195.9 36.4 %copy-start.33 = (f32[1,1,300,300]{3,1,2,0:T(1,128)S(1)}, f32[1,1,300,300]{3,1,2,0:T(1,128)}, u32[]{:S(2)}) copy-start(f32[1,1,300,300]{3,1,2,0:T(1,128)} %get-tuple-element.115) | copy-start | bytes 1080004
  195.9 36.4 %copy-start.87 = (f32[128]{0:T(128)S(1)}, f32[128]{0:T(128)}, u32[]{:S(2)}) copy-start(f32[128]{0:T(128)} %copy-done.86) | copy-start | bytes 1540
  195.9 36.4 %copy-start.92 = (f32[128]{0:T(128)S(1)}, f32[128]{0:T(128)}, u32[]{:S(2)}) copy-start(f32[128]{0:T(128)} %copy-done.91) | copy-start | bytes 1540
  197.0 37.1 %copy-start.116 = (f32[128]{0:T(128)S(1)}, f32[128]{0:T(128)}, u32[]{:S(2)}) copy-start(f32[128]{0:T(128)} %copy-done.115) | copy-start | bytes 1540
  200.6 90.1 %all-reduce.27.cloned.1.call-start = ((), (), s32[]{:S(2)}) async-start(), calls=%async_computation.3 | async-start | bytes 311296 | tf_op jit(solution)/shard_map/psum | solution.py:144
  259.0 304.4 %all-reduce.31.cloned.1.call-start = ((), (), s32[]{:S(2)}) async-start(), calls=%async_computation.5 | async-start | bytes 16187392 | tf_op jit(solution)/shard_map/psum | solution.py:183
  264.9 25.7 %copy-start.68 = (f32[128,300]{0,1:T(8,128)S(1)}, f32[128,300]{0,1:T(8,128)}, u32[]{:S(2)}) copy-start(f32[128,300]{0,1:T(8,128)} %param.13) | copy-start | bytes 460804
  293.2 411.6 %all-reduce.29.cloned.1.call-start = ((), (), s32[]{:S(2)}) async-start(), calls=%async_computation.4 | async-start | bytes 5603328 | tf_op jit(solution)/shard_map/psum | solution.py:195
  395.8 43.1 %copy-start.69 = (f32[128,300]{0,1:T(8,128)S(1)}, f32[128,300]{0,1:T(8,128)}, u32[]{:S(2)}) copy-start(f32[128,300]{0,1:T(8,128)} %all-reduce.27.cloned.1.call-done) | copy-start | bytes 460804
  395.8 82.5 %copy-start.31 = (f32[1,1,300,300]{3,1,2,0:T(1,128)S(1)}, f32[1,1,300,300]{3,1,2,0:T(1,128)}, u32[]{:S(2)}) copy-start(f32[1,1,300,300]{3,1,2,0:T(1,128)} %copy-done.30) | copy-start | bytes 1080004
  (100 other events, 337.7 us)
Sparse Core Ops, SparseCore 0:
  51.0 31.6 all-reduce.20
  133.9 31.8 all-reduce.22
  200.7 31.5 all-reduce.24
  259.1 31.5 all-reduce.26
  295.7 267.6 all-reduce.30
  569.3 135.3 all-reduce.28
where the time goes:
time: 737 us; the launch traced here: 727 us
  waiting for transfers between devices  289 us (39%)
  blocking collectives  128 us (17%)
  local copies, waits for them, and re-layouts  125 us (17%)
  matrix products  90.8 us (12%)
  other arithmetic  77.4 us (11%)
  between operations  16.1 us (2%)
    psum x1, waiting for transfers between devices, on_device(): leaf_sum = lax.psum((leaf_stack[0], leaf_stack[1]), ('graphs', 'leaves'))  140 us
    dot_general x42, matrix products, matmul_hi(): return jnp.dot(left, right, precision=precise)  90.8 us
    psum x1, waiting for transfers between devices, on_device(): lax.psum((center_stack[0], center_stack[1], center_stack[2], center_stack...  83.9 us
    psum x2, waiting for transfers between devices, on_device(): grad_queries = lax.psum(query_part, 'leaves')  53.4 us
    psum x1, blocking collectives, on_device(): leaf_sum = lax.psum((leaf_stack[0], leaf_stack[1]), ('graphs', 'leaves'))  40.8 us
    psum x1, blocking collectives, on_device(): lax.psum((center_stack[0], center_stack[1], center_stack[2], center_stack...  38.6 us
    unnamed x253, local copies, waits for them, and re-layouts  30.6 us
    psum x2, blocking collectives, on_device(): lax.psum((local_sum * jnp.repeat(factor, HEAD_DIM, axis=-1), local_total...  25 us
  transfers between devices with their start and end apart: 6, of which 5 were waited for; matrix products, arithmetic and copies ran while one was open for 22% of the time, Pallas kernels for 0%

commit v1 on v0

v1 whole, which is shorter than its diff:
```python
import functools

import jax
import jax.numpy as jnp
from jax import lax
from jax.experimental import pallas as pl
from jax.experimental.pallas import tpu as pltpu
from jax.sharding import PartitionSpec as P

HEADS = 12
HEAD_DIM = 25
LAYERS = 2
LANES = 128
ROWS = 8
HEAD_ROWS = 16
EPS = 1e-05
SCALE = HEAD_DIM ** (-0.5)
GELU_A = 0.7978845608028654
GELU_B = 0.044715

F32 = jnp.float32
BF16 = jnp.bfloat16
NN = (((1,), (0,)), ((), ()))
TN = (((0,), (0,)), ((), ()))
NT = (((1,), (1,)), ((), ()))
BOTH = ("graphs", "leaves")
VMEM = pl.BlockSpec(memory_space=pltpu.VMEM)
SMEM = pl.BlockSpec(memory_space=pltpu.SMEM)


def ceil_div(a, b):
    return -(-a // b)


def dot(a, b, dims):
    return lax.dot_general(a, b, dims, preferred_element_type=F32)


def split(v):
    high = v.astype(BF16)
    return high, (v - high.astype(F32)).astype(BF16)


def mul_pair(a, b, dims):
    return dot(a[0], b[0], dims) + (dot(a[0], b[1], dims) + dot(a[1], b[0], dims))


def mul_narrow(a, b, dims):
    width = b[0].shape[1]
    both = dot(a[0], jnp.concatenate(b, axis=1), dims)
    return both[:, :width] + (both[:, width:] + dot(a[1], b[0], dims))


def outer(a, b):
    left = jnp.concatenate([a[0], a[0], a[1]], axis=1)
    right = jnp.concatenate([b[0], b[1], b[0]], axis=1)
    return dot(left, right, NT)


def lane_sums(v):
    ones = jnp.ones((ROWS, v.shape[1]), BF16)
    high, low = split(v)
    return (dot(ones, high, NT) + dot(ones, low, NT))[0:1, :]


def columns(rows):
    count = rows.shape[0]
    if count % ROWS:
        fill = jnp.zeros((ROWS - count % ROWS, rows.shape[1]), F32)
        rows = jnp.concatenate([rows, fill], axis=0)
    return rows.T


def slot_cols(ref, slots):
    return jnp.concatenate([ref[:, s, :] for s in range(slots)], axis=1)


def leaf_forward(m, square_ref, bias_ref, layer, k_ref, v_ref):
    pair = split(m)
    cols = columns(bias_ref[:, layer, :])
    k_ref[...] = mul_pair(split(square_ref[layer, :, 1, :].T), pair, NN)
    v_ref[...] = mul_pair(split(square_ref[layer, :, 2, :].T), pair, NN) + cols[:, 5:6]
    return mul_pair(split(square_ref[layer, :, 3, :].T), pair, NN) + cols[:, 6:7]


def attend(q_ref, k_ref, v_ref, live, s_ref, w_ref, part_ref):
    slots = len(live)
    s_ref[...] = jnp.zeros(s_ref.shape, F32)
    for h in range(HEADS):
        at = slice(HEAD_DIM * h, HEAD_DIM * (h + 1))
        q = q_ref[at, :]
        for s in range(slots):
            k = k_ref[at, LANES * s : LANES * (s + 1)]
            s_ref[s, h : h + 1, :] = jnp.sum(q * k, axis=0, keepdims=True)
    scores = [jnp.where(live[s], s_ref[s] * SCALE, -1e30) for s in range(slots)]
    top = functools.reduce(jnp.maximum, scores)
    weights = [jnp.where(live[s], jnp.exp(scores[s] - top), 0.0) for s in range(slots)]
    for s in range(slots):
        s_ref[s] = scores[s]
        w_ref[s] = weights[s]
    for h in range(HEADS):
        at = slice(HEAD_DIM * h, HEAD_DIM * (h + 1))
        total = 0.0
        for s in range(slots):
            total += w_ref[s, h : h + 1, :] * v_ref[at, LANES * s : LANES * (s + 1)]
        part_ref[at, :] = total
    width = HEADS * HEAD_DIM
    base = ceil_div(width, ROWS) * ROWS
    part_ref[width:base, :] = jnp.zeros((base - width, LANES), F32)
    part_ref[base : base + HEAD_ROWS, :] = functools.reduce(jnp.add, weights)
    part_ref[base + HEAD_ROWS : base + 2 * HEAD_ROWS, :] = top


def tree(values, op):
    while len(values) > 1:
        values = [op(values[i], values[i + 1]) for i in range(0, len(values), 2)]
    return values[0]


def combine(part_refs, r_ref, att_ref, top_ref, total_ref):
    base = ceil_div(HEADS * HEAD_DIM, ROWS) * ROWS
    totals = [ref[base : base + HEAD_ROWS, :] for ref in part_refs]
    tops = [ref[base + HEAD_ROWS : base + 2 * HEAD_ROWS, :] for ref in part_refs]
    top = tree(tops, jnp.maximum)
    factors = [jnp.exp(t - top) for t in tops]
    total = tree([a * b for a, b in zip(totals, factors)], jnp.add)
    head = lax.broadcasted_iota(jnp.int32, total.shape, 0) < HEADS
    total = jnp.where(head, total, 1.0)
    top_ref[...] = top
    total_ref[...] = total
    for n, factor in enumerate(factors):
        r_ref[n] = factor / total
    for h in range(HEADS):
        at = slice(HEAD_DIM * h, HEAD_DIM * (h + 1))
        att_ref[at, :] = tree(
            [ref[at, :] * r_ref[n, h : h + 1, :] for n, ref in enumerate(part_refs)], jnp.add
        )


def normalise(v):
    centred = v - jnp.mean(v, axis=0, keepdims=True)
    spread = lax.rsqrt(jnp.mean(centred * centred, axis=0, keepdims=True) + EPS)
    return centred * spread, spread


def normalise_back(grad, gain, unit, spread):
    g = grad * gain
    return spread * (
        g - jnp.mean(g, axis=0, keepdims=True) - unit * jnp.mean(g * unit, axis=0, keepdims=True)
    )


def gelu_tanh(z):
    return jnp.tanh(GELU_A * (z + GELU_B * (z * z * z)))


def gelu(z, t):
    return 0.5 * z * (1.0 + t)


def gelu_slope(z, t):
    return 0.5 * (1.0 + t) + 0.5 * z * (1.0 - t * t) * (GELU_A * (1.0 + 3.0 * GELU_B * (z * z)))


def center_forward(att, states, out_ref, in_ref, down_ref, hid_ref, bias_ref, gain_ref, layer):
    cols = columns(bias_ref[:, layer, :])
    gains = columns(gain_ref[layer, :, :])
    hid = columns(hid_ref[layer : layer + 1, :])
    o = mul_narrow(split(out_ref[:, layer, :].T), split(att), NN) + cols[:, 1:2]
    unit1, spread1 = normalise(states + o)
    h1 = unit1 * gains[:, 0:1] + cols[:, 2:3]
    z = mul_narrow(split(in_ref[:, layer, :].T), split(h1), NN) + hid[:, 0:1]
    u = gelu(z, gelu_tanh(z))
    f = mul_narrow(split(down_ref[:, layer, :]), split(u), NN) + cols[:, 3:4]
    unit2, spread2 = normalise(h1 + f)
    return unit1, spread1, z, unit2, spread2, unit2 * gains[:, 1:2] + cols[:, 4:5]


def extend(ref, value):
    rows, width = ref.shape[0], value.shape[0]
    ref[width:rows, :] = jnp.where(
        lax.broadcasted_iota(jnp.int32, (rows - width, value.shape[1]), 0) == 0, 1.0, 0.0
    )
    ref[0:width, :] = value


class Plan:
    def __init__(self, width, hidden, graph_devices, leaf_devices):
        self.width, self.hidden = width, hidden
        self.graph_devices, self.leaf_devices = graph_devices, leaf_devices
        self.row_tiles = ceil_div(width + 4, ROWS)
        self.share = ceil_div(self.row_tiles, leaf_devices)
        self.share_rows = self.share * ROWS
        self.hid_full, self.hid_tail = divmod(hidden, LANES)
        self.wid_full, self.wid_tail = divmod(width, LANES)
        self.center_lanes = 2 * self.hid_full + 1 + self.wid_full + 1
        self.center_tiles = ceil_div(self.share * self.center_lanes, graph_devices)
        self.query_lanes = self.wid_full + 1
        self.query_tiles = ceil_div(self.share * self.query_lanes, graph_devices)
        self.leaf_lanes = 3 * self.wid_full + 2
        self.leaf_tiles = ceil_div(self.row_tiles * self.leaf_lanes, graph_devices * leaf_devices)
        self.chunk_tiles = self.center_tiles + self.query_tiles + self.leaf_tiles
        self.last_owner, self.last_tile = divmod(width // ROWS, self.share)
        self.last_row = width % ROWS


def joint_tail(left, right, width):
    lane = lax.broadcasted_iota(jnp.int32, left.shape, 1)
    return jnp.where(lane < width, left, pltpu.roll(right, width, 1))


def deal(tiles, per_chunk, abs_ref):
    for t, tile in enumerate(tiles):
        chunk, at = divmod(t, per_chunk)
        abs_ref[chunk, at * ROWS : (at + 1) * ROWS, :] = tile
    for t in range(len(tiles), per_chunk * abs_ref.shape[0]):
        chunk, at = divmod(t, per_chunk)
        abs_ref[chunk, at * ROWS : (at + 1) * ROWS, :] = jnp.zeros((ROWS, LANES), F32)


def send_graphs(abs_ref, me, keep_ref, give_ref):
    half = keep_ref.shape[0]
    for r in range(half):
        keep_ref[r] = abs_ref[jnp.bitwise_xor(2 * r, me)]
        give_ref[r] = abs_ref[jnp.bitwise_xor(2 * r + 1, me)]


def center_backward(
    plan, grad, att, states, z, unit1, spread1, unit2, spread2,
    out_ref, in_ref, down_ref, bias_ref, gain_ref, layer, me_graph, me_leaf,
    ext_ref, wide1_ref, wide2_ref, abs_ref, keep_ref, give_ref,
):
    cols = columns(bias_ref[:, layer, :])
    gains = columns(gain_ref[layer, :, :])
    share = pl.ds(pl.multiple_of(me_leaf * plan.share_rows, ROWS), plan.share_rows)
    width, hidden = plan.width, plan.hidden

    g_f = normalise_back(grad, gains[:, 1:2], unit2, spread2)
    t = gelu_tanh(z)
    u = gelu(z, t)
    pair_f = split(g_f)
    dz = mul_narrow(split(down_ref[:, layer, :].T), pair_f, NN) * gelu_slope(z, t)
    pair_z = split(dz)
    g_h1 = g_f + mul_narrow(split(in_ref[:, layer, :]), pair_z, NN)
    g_o = normalise_back(g_h1, gains[:, 0:1], unit1, spread1)
    pair_o = split(g_o)
    g_att = mul_narrow(split(out_ref[:, layer, :]), pair_o, NN)

    extend(ext_ref, unit1 * gains[:, 0:1] + cols[:, 2:3])
    wide1_ref[:, 0:hidden] = outer(split(ext_ref[share, :]), pair_z)
    extend(ext_ref, g_f)
    wide2_ref[:, 0:hidden] = outer(split(ext_ref[share, :]), split(u))
    extend(ext_ref, att)
    own_out = outer(split(ext_ref[share, :]), pair_o)

    sums = [lane_sums(v) for v in (g_h1, g_h1 * unit1, g_f, grad, grad * unit2)]
    row = plan.last_tile * ROWS + plan.last_row

    @pl.when(me_leaf == plan.last_owner)
    def _():
        wide2_ref[row + 1 : row + 2, 0:width] = sums[3]
        wide2_ref[row + 2 : row + 3, 0:width] = sums[4]

    tiles = []
    for r in range(plan.share):
        at = slice(r * ROWS, (r + 1) * ROWS)
        for ref in (wide1_ref, wide2_ref):
            tiles += [ref[at, LANES * c : LANES * (c + 1)] for c in range(plan.hid_full)]
        tail = slice(LANES * plan.hid_full, LANES * (plan.hid_full + 1))
        tiles.append(joint_tail(wide1_ref[at, tail], wide2_ref[at, tail], plan.hid_tail))
        for c in range(plan.wid_full + 1):
            tiles.append((r, c))
    wide1_ref[:, 0:width] = own_out

    @pl.when(me_leaf == plan.last_owner)
    def _():
        for n in range(3):
            wide1_ref[row + 1 + n : row + 2 + n, 0:width] = sums[n]

    tiles = [
        wide1_ref[t[0] * ROWS : (t[0] + 1) * ROWS, LANES * t[1] : LANES * (t[1] + 1)]
        if isinstance(t, tuple)
        else t
        for t in tiles
    ]
    deal(tiles, plan.center_tiles, abs_ref)
    send_graphs(abs_ref, me_graph, keep_ref, give_ref)
    return g_att, g_o


def attend_back(att_ref, gatt_ref, q_ref, k_ref, v_ref, s_ref, top, total, slots, ct_ref, p_ref, gq_ref, gk_ref, gv_ref):
    for s in range(slots):
        p_ref[s] = jnp.exp(s_ref[s] - top) / total
    for h in range(HEADS):
        at = slice(HEAD_DIM * h, HEAD_DIM * (h + 1))
        ga, q = gatt_ref[at, :], q_ref[at, :]
        centre = jnp.sum(ga * att_ref[at, :], axis=0, keepdims=True)
        gq = 0.0
        for s in range(slots):
            lanes = slice(LANES * s, LANES * (s + 1))
            k = k_ref[at, lanes]
            p = p_ref[s, h : h + 1, :]
            gp = jnp.sum(ga * v_ref[at, lanes], axis=0, keepdims=True)
            gs = p * (gp - centre) * SCALE
            gv_ref[at, lanes] = p * ga
            gk_ref[at, lanes] = gs * q
            gq += gs * k
        gq_ref[at, :] = gq


def query_gradient(plan, states, gq, me_graph, me_leaf, ext_ref, wide_ref, abs_ref, keep_ref, give_ref):
    share = pl.ds(pl.multiple_of(me_leaf * plan.share_rows, ROWS), plan.share_rows)
    extend(ext_ref, states)
    wide_ref[:, 0 : plan.width] = outer(split(ext_ref[share, :]), split(gq))
    tiles = [
        wide_ref[r * ROWS : (r + 1) * ROWS, LANES * c : LANES * (c + 1)]
        for r in range(plan.share)
        for c in range(plan.query_lanes)
    ]
    deal(tiles, plan.query_tiles, abs_ref)
    send_graphs(abs_ref, me_graph, keep_ref, give_ref)


def live_rows(me_ref, count_ref, slots):
    first = me_ref[1] * slots
    return [count_ref[...] > first + s for s in range(slots)]


def first_kernel(slots, me_ref, count_ref, x_ref, e_ref, h_ref, square_ref, bias_ref,
                 part_ref, q_ref, k_ref, v_ref, s_ref, e1_ref, w_ref):
    cols = columns(bias_ref[:, 0, :])
    m = slot_cols(x_ref, slots) * slot_cols(e_ref, slots)
    q_ref[...] = mul_narrow(split(square_ref[0, :, 0, :].T), split(h_ref[...]), NN) + cols[:, 0:1]
    step = leaf_forward(m, square_ref, bias_ref, 0, k_ref, v_ref)
    for s in range(slots):
        e1_ref[:, s, :] = e_ref[:, s, :] + step[:, LANES * s : LANES * (s + 1)]
    attend(q_ref, k_ref, v_ref, live_rows(me_ref, count_ref, slots), s_ref, w_ref, part_ref)


def second_kernel(slots, x_ref, e1_ref, square_ref, bias_ref, k_ref, v_ref, e2_ref):
    m = slot_cols(x_ref, slots) * slot_cols(e1_ref, slots)
    step = leaf_forward(m, square_ref, bias_ref, 1, k_ref, v_ref)
    for s in range(slots):
        e2_ref[:, s, :] = e1_ref[:, s, :] + step[:, LANES * s : LANES * (s + 1)]


def third_kernel(slots, me_ref, count_ref, p0, p1, p2, p3, h_ref, k_ref, v_ref, square_ref, out_ref, in_ref, down_ref,
                 hid_ref, bias_ref, gain_ref,
                 part_ref, att_ref, top_ref, total_ref, unit1_ref, spread1_ref, z_ref, unit2_ref, spread2_ref, h2_ref,
                 q_ref, s_ref, r_ref, w_ref):
    combine([p0, p1, p2, p3], r_ref, att_ref, top_ref, total_ref)
    unit1, spread1, z, unit2, spread2, h2 = center_forward(
        att_ref[...], h_ref[...], out_ref, in_ref, down_ref, hid_ref, bias_ref, gain_ref, 0
    )
    unit1_ref[...] = unit1
    spread1_ref[...] = spread1
    z_ref[...] = z
    unit2_ref[...] = unit2
    spread2_ref[...] = spread2
    h2_ref[...] = h2
    cols = columns(bias_ref[:, 1, :])
    q_ref[...] = mul_narrow(split(square_ref[1, :, 0, :].T), split(h2), NN) + cols[:, 0:1]
    attend(q_ref, k_ref, v_ref, live_rows(me_ref, count_ref, slots), s_ref, w_ref, part_ref)


def fourth_kernel(plan, slots, me_ref, p0, p1, p2, p3, h_ref, q_ref, k_ref, v_ref, s_ref, cot_ref, out_ref, in_ref,
                  down_ref, hid_ref, bias_ref, gain_ref,
                  center_ref, gq_ref, gk_ref, gv_ref, res_ref, keep_ref, give_ref,
                  r_ref, att_ref, top_ref, total_ref, gatt_ref, p_ref, ext_ref, wide1_ref, wide2_ref, abs_ref):
    combine([p0, p1, p2, p3], r_ref, att_ref, top_ref, total_ref)
    unit1, spread1, z, unit2, spread2, out = center_forward(
        att_ref[...], h_ref[...], out_ref, in_ref, down_ref, hid_ref, bias_ref, gain_ref, 1
    )
    center_ref[...] = out
    gatt_ref[...], res_ref[...] = center_backward(
        plan, cot_ref[...], att_ref[...], h_ref[...], z, unit1, spread1, unit2, spread2,
        out_ref, in_ref, down_ref, bias_ref, gain_ref, 1, me_ref[0], me_ref[1],
        ext_ref, wide1_ref, wide2_ref, abs_ref, keep_ref, give_ref,
    )
    attend_back(att_ref, gatt_ref, q_ref, k_ref, v_ref, s_ref, top_ref[...], total_ref[...], slots,
                None, p_ref, gq_ref, gk_ref, gv_ref)


def fifth_kernel(plan, slots, layer, last, me_ref, x_ref, e_ref, ge_ref, *refs):
    if last:
        gx_ref, *refs = refs
    (gk_ref, gv_ref, square_ref, new_gx_ref, new_ge_ref, core_ref, give_ref, keep_ref, ext_ref, wide_ref, abs_ref) = refs
    extend(ext_ref, slot_cols(x_ref, slots) * slot_cols(e_ref, slots))
    ge = slot_cols(ge_ref, slots)
    pairs = [split(v) for v in (gk_ref[...], gv_ref[...], ge)]
    gm = tree([mul_pair(split(square_ref[layer, :, n + 1, :]), pairs[n], NN) for n in range(2)], jnp.add)
    gm = gm + mul_pair(split(square_ref[layer, :, 3, :]), pairs[2], NN)
    for s in range(slots):
        part = gm[:, LANES * s : LANES * (s + 1)]
        gx = part * e_ref[:, s, :]
        new_gx_ref[:, s, :] = gx_ref[:, s, :] + gx if last else gx
        new_ge_ref[:, s, :] = ge_ref[:, s, :] + part * x_ref[:, s, :]
    m = split(ext_ref[...])
    for n in range(3):
        wide_ref[n, :, 0 : plan.width] = outer(m, pairs[n])
    tiles = []
    for r in range(plan.row_tiles):
        at = slice(r * ROWS, (r + 1) * ROWS)
        for n in range(3):
            tiles += [wide_ref[n, at, LANES * c : LANES * (c + 1)] for c in range(plan.wid_full)]
        tail = slice(LANES * plan.wid_full, LANES * (plan.wid_full + 1))
        tiles.append(joint_tail(wide_ref[0, at, tail], wide_ref[1, at, tail], plan.wid_tail))
        tiles.append(wide_ref[2, at, tail])
    deal(tiles, plan.leaf_tiles, abs_ref)
    me_graph, me_leaf = me_ref[0], me_ref[1]
    half = plan.graph_devices // 2
    for other in range(plan.leaf_devices):
        leaf = jnp.bitwise_xor(other, me_leaf)
        for r in range(plan.graph_devices):
            rel = 2 * (r % half) + r // half
            source = abs_ref[jnp.bitwise_xor(rel, me_graph) * plan.leaf_devices + leaf]
            if other % 2:
                core_ref[other // 2, r] = source
            elif other // 2:
                give_ref[r] = source
            else:
                keep_ref[r] = source


def sixth_kernel(plan, slots, me_ref, g0, g1, g2, g3, res_ref, h2_ref, square_ref,
                 att_ref, h_ref, z_ref, unit1_ref, spread1_ref, unit2_ref, spread2_ref, top_ref, total_ref,
                 q_ref, k_ref, v_ref, s_ref, out_ref, in_ref, down_ref, bias_ref, gain_ref,
                 gq_ref, gk_ref, gv_ref, new_res_ref, keep_ref, give_ref, q_keep_ref, q_give_ref,
                 gatt_ref, p_ref, ext_ref, wide1_ref, wide2_ref, abs_ref, q_abs_ref):
    gq = tree([ref[...] for ref in (g0, g1, g2, g3)], jnp.add)
    grad = res_ref[...] + mul_narrow(split(square_ref[1, :, 0, :]), split(gq), NN)
    query_gradient(plan, h2_ref[...], gq, me_ref[0], me_ref[1], ext_ref, wide1_ref, q_abs_ref, q_keep_ref, q_give_ref)
    gatt_ref[...], new_res_ref[...] = center_backward(
        plan, grad, att_ref[...], h_ref[...], z_ref[...], unit1_ref[...], spread1_ref[...], unit2_ref[...],
        spread2_ref[...], out_ref, in_ref, down_ref, bias_ref, gain_ref, 0, me_ref[0], me_ref[1],
        ext_ref, wide1_ref, wide2_ref, abs_ref, keep_ref, give_ref,
    )
    attend_back(att_ref, gatt_ref, q_ref, k_ref, v_ref, s_ref, top_ref[...], total_ref[...], slots,
                None, p_ref, gq_ref, gk_ref, gv_ref)


def seventh_kernel(plan, me_ref, g0, g1, g2, g3, res_ref, h_ref, square_ref,
                   grad_ref, keep_ref, give_ref, ext_ref, wide_ref, abs_ref):
    gq = tree([ref[...] for ref in (g0, g1, g2, g3)], jnp.add)
    grad_ref[...] = res_ref[...] + mul_narrow(split(square_ref[0, :, 0, :]), split(gq), NN)
    query_gradient(plan, h_ref[...], gq, me_ref[0], me_ref[1], ext_ref, wide_ref, abs_ref, keep_ref, give_ref)


def last_kernel(plan, routes, me_ref, *refs):
    pieces = [refs[len(routes) * layer : len(routes) * (layer + 1)] for layer in range(LAYERS)]
    square_ref, out_ref, in_ref, down_ref, hid_ref, bias_ref, gain_ref, all_ref = refs[len(routes) * LAYERS :]
    me_graph, me_leaf = me_ref[0], me_ref[1]
    width, hidden = plan.width, plan.hidden
    for layer in range(LAYERS):
        for ref, (graph_bits, leaf, first, rows) in zip(pieces[layer], routes):
            for n, graph in enumerate(graph_bits):
                all_ref[
                    jnp.bitwise_xor(graph, me_graph), jnp.bitwise_xor(leaf, me_leaf), first : first + rows, :
                ] = ref[n]

        def tile(kind, index):
            per = (plan.center_tiles, plan.query_tiles, plan.leaf_tiles)[kind]
            base = (0, plan.center_tiles, plan.center_tiles + plan.query_tiles)[kind]
            leaf, index = index if kind < 2 else (None, index)
            chunk, at = divmod(index, per)
            if kind == 2:
                chunk, leaf = divmod(chunk, plan.leaf_devices)
            at = (base + at) * ROWS
            return all_ref[chunk, leaf, at : at + ROWS, :]

        hid_tail, wid_tail = plan.hid_tail, plan.wid_tail
        for r in range(plan.row_tiles):
            leaf, own = divmod(r, plan.share)
            rows = min(ROWS, width - r * ROWS)
            at = slice(r * ROWS, r * ROWS + rows)
            center = [tile(0, (leaf, own * plan.center_lanes + c)) for c in range(plan.center_lanes)]
            query = [tile(1, (leaf, own * plan.query_lanes + c)) for c in range(plan.query_lanes)]
            sides = [tile(2, r * plan.leaf_lanes + c) for c in range(plan.leaf_lanes)]
            full, wid = plan.hid_full, plan.wid_full
            tail = center[2 * full]
            ins = center[:full] + [tail]
            downs = center[full : 2 * full] + [pltpu.roll(tail, LANES - hid_tail, 1)]
            outs = center[2 * full + 1 :]
            joint = sides[3 * wid]
            keys = sides[:wid] + [joint]
            values = sides[wid : 2 * wid] + [pltpu.roll(joint, LANES - wid_tail, 1)]
            sides_e = sides[2 * wid : 3 * wid] + [sides[3 * wid + 1]]
            for c in range(full + 1):
                count = LANES if c < full else hid_tail
                lanes = slice(LANES * c, LANES * c + count)
                in_ref[at, layer, lanes] = ins[c][:rows, :count]
                down_ref[at, layer, lanes] = downs[c][:rows, :count]
            for c in range(wid + 1):
                count = LANES if c < wid else wid_tail
                lanes = slice(LANES * c, LANES * c + count)
                out_ref[at, layer, lanes] = outs[c][:rows, :count]
                for n, part in enumerate((query, keys, values, sides_e)):
                    square_ref[layer, at, n, lanes] = part[c][:rows, :count]
            if r == width // ROWS:
                first = plan.last_row
                for c in range(full + 1):
                    count = LANES if c < full else hid_tail
                    lanes = slice(LANES * c, LANES * c + count)
                    hid_ref[layer : layer + 1, lanes] = ins[c][first : first + 1, :count]
                for c in range(wid + 1):
                    count = LANES if c < wid else wid_tail
                    lanes = slice(LANES * c, LANES * c + count)
                    found = (
                        (query, 0), (outs, 0), (outs, 1), (outs, 3), (downs, 1), (values, 0), (sides_e, 0),
                    )
                    for n, (part, row) in enumerate(found):
                        bias_ref[n, layer : layer + 1, lanes] = part[c][first + row : first + row + 1, :count]
                    gain_ref[layer, 0:1, lanes] = outs[c][first + 2 : first + 3, :count]
                    gain_ref[layer, 1:2, lanes] = downs[c][first + 2 : first + 3, :count]


def swap(values, axis, size, distance):
    pairs = [(i, i ^ distance) for i in range(size)]
    return jax.tree.map(lambda v: lax.ppermute(v, axis, pairs), values)


def bit_groups(size):
    bits, groups = size.bit_length() - 1, []
    at = bits
    while at > 1:
        low = max(1, at - 2)
        groups.append((low, at - low))
        at = low
    return groups


def graph_scatter(keep, give, size):
    got = swap(give, "graphs", size, 1)
    held = [keep, got]
    half = size // 2
    for low, count in bit_groups(size):
        ways = 1 << count
        step = half // ways
        parts = [tree([v[step * k : step * (k + 1)] for v in held], jnp.add) if len(held) in (1, 2, 4) else None for k in range(ways)]
        held = [parts[0]] + [swap(parts[k], "graphs", size, k << low) for k in range(1, ways)]
        half = step
    return tree(held, jnp.add)[0]


def leaf_scatter(core, give, keep, sizes):
    got = swap(core, "leaves", sizes[1], 1)
    far = swap(give + got[1], "leaves", sizes[1], 2)
    half = sizes[0] // 2
    even = (keep[:half] + got[0, :half]) + far[:half]
    odd = (keep[half:] + got[0, half:]) + far[half:]
    return graph_scatter(even, odd, sizes[0])


def gather(chunk, sizes):
    graph_devices, leaf_devices = sizes
    held = [chunk]
    graphs = [0]
    for low, count in reversed(bit_groups(graph_devices)):
        ways = 1 << count
        held = held + [swap(v, "graphs", graph_devices, k << low) for k in range(1, ways) for v in held]
        graphs = graphs + [g ^ (k << low) for k in range(1, ways) for g in graphs]
    rows = chunk.shape[0]
    middle = rows // 2 // ROWS * ROWS
    pieces, routes = [], []
    for n, (first, last) in enumerate(((0, middle), (middle, rows))):
        block = jnp.stack([v[first:last] for v in held])
        parts = [(block, 0, 0)]
        for turn in (0, 1) if n else (1, 0):
            if turn:
                parts = parts + [(swap(v, "graphs", graph_devices, 1), g ^ 1, f) for v, g, f in parts]
            else:
                parts = parts + [(swap(v, "leaves", leaf_devices, 2), g, f ^ 2) for v, g, f in parts]
        parts = parts + [(swap(v, "leaves", leaf_devices, 1), g, f ^ 1) for v, g, f in parts]
        pieces += [v for v, _, _ in parts]
        routes += [(tuple(x ^ g for x in graphs), f, first, last - first) for _, g, f in parts]
    return pieces, routes


def on_device(
    sizes,
    centers,
    leaf_nodes,
    edges,
    leaf_counts,
    square,
    out_proj,
    ff_in,
    ff_out,
    ff_bias,
    biases,
    gains,
    cot_center,
    cot_edges,
):
    graphs, slots, width = leaf_nodes.shape
    hidden = ff_in.shape[2]
    graph_devices, leaf_devices = sizes
    plan = Plan(width, hidden, graph_devices, leaf_devices)
    me = jnp.stack([lax.axis_index("graphs"), lax.axis_index("leaves")]).astype(jnp.int32)

    h = centers.T
    x = leaf_nodes.transpose(2, 1, 0)
    e = edges.transpose(2, 1, 0)
    count = leaf_counts.reshape(1, graphs)
    sq = square.transpose(0, 2, 1, 3)
    wo = out_proj.transpose(1, 0, 2)
    w1 = ff_in.transpose(1, 0, 2)
    w2 = ff_out.transpose(2, 0, 1)
    bias = biases.transpose(1, 0, 2)
    gc = cot_center.T
    ge = cot_edges.transpose(2, 1, 0)

    base = ceil_div(width, ROWS) * ROWS
    wide = plan.share_rows
    lanes = ceil_div(hidden, LANES) * LANES
    shape = lambda *s: jax.ShapeDtypeStruct(s, F32)
    scratch = lambda *s: pltpu.VMEM(s, F32)
    cell = (width, graphs)
    row = (1, graphs)
    sides = (width, slots * graphs)
    cube = (width, slots, graphs)
    heads = (HEAD_ROWS, graphs)
    scores = (slots, HEAD_ROWS, graphs)
    part = (base + 2 * HEAD_ROWS, graphs)
    half = graph_devices // 2

    def call(kernel, ins, outs, scratches, first_smem=True, flops=0):
        return pl.pallas_call(
            kernel,
            in_specs=[SMEM if first_smem and n == 0 else VMEM for n in range(len(ins))],
            out_specs=[VMEM] * len(outs),
            out_shape=[shape(*s) for s in outs],
            scratch_shapes=[scratch(*s) for s in scratches],
            compiler_params=pltpu.CompilerParams(vmem_limit_bytes=56 << 20),
            cost_estimate=pl.CostEstimate(flops=flops, bytes_accessed=0, transcendentals=0),
        )(*ins)

    def around(value):
        return [value] + [swap(value, "leaves", leaf_devices, k) for k in range(1, leaf_devices)]

    part1, q1, k1, v1, s1, e1 = call(
        functools.partial(first_kernel, slots),
        (me, count, x, e, h, sq, bias),
        (part, cell, sides, sides, scores, cube),
        (scores,),
    )
    parts1 = around(part1)
    k2, v2, e2 = call(
        functools.partial(second_kernel, slots), (x, e1, sq, bias), (sides, sides, cube), (), first_smem=False
    )
    part2, att1, top1, total1, unit1, spread1, z1, unit2, spread2, h2, q2, s2 = call(
        functools.partial(third_kernel, slots),
        (me, count, *parts1, h, k2, v2, sq, wo, w1, w2, ff_bias, bias, gains),
        (part, cell, heads, heads, cell, row, (hidden, graphs), cell, row, cell, cell, scores),
        ((leaf_devices, *heads), scores),
    )
    parts2 = around(part2)
    center_chunk = (half, plan.center_tiles * ROWS, LANES)
    query_chunk = (half, plan.query_tiles * ROWS, LANES)
    leaf_chunk = (graph_devices, plan.leaf_tiles * ROWS, LANES)
    ext = (wide * leaf_devices, graphs)
    center_out, gq2, gk2, gv2, res2, keep2, give2 = call(
        functools.partial(fourth_kernel, plan, slots),
        (me, *parts2, h2, q2, k2, v2, s2, gc, wo, w1, w2, ff_bias, bias, gains),
        (cell, cell, sides, sides, cell, center_chunk, center_chunk),
        ((leaf_devices, *heads), cell, heads, heads, cell, scores, ext, (wide, lanes), (wide, lanes),
         (graph_devices, *center_chunk[1:])),
    )
    gqs2 = around(gq2)
    leaf_scratch = (
        (plan.row_tiles * ROWS, slots * graphs),
        (3, plan.row_tiles * ROWS, ceil_div(width, LANES) * LANES),
        (graph_devices * leaf_devices, *leaf_chunk[1:]),
    )
    gx2, ge1, lcore2, lgive2, lkeep2 = call(
        functools.partial(fifth_kernel, plan, slots, 1, False),
        (me, x, e1, ge, gk2, gv2, sq),
        (cube, cube, (2, *leaf_chunk), leaf_chunk, leaf_chunk),
        leaf_scratch,
    )
    gq1, gk1, gv1, res1, keep1, give1, qkeep2, qgive2 = call(
        functools.partial(sixth_kernel, plan, slots),
        (me, *gqs2, res2, h2, sq, att1, h, z1, unit1, spread1, unit2, spread2, top1, total1,
         q1, k1, v1, s1, wo, w1, w2, bias, gains),
        (cell, sides, sides, cell, center_chunk, center_chunk, query_chunk, query_chunk),
        (cell, scores, ext, (wide, lanes), (wide, lanes),
         (graph_devices, *center_chunk[1:]), (graph_devices, *query_chunk[1:])),
    )
    gqs1 = around(gq1)
    gx1, ge0, lcore1, lgive1, lkeep1 = call(
        functools.partial(fifth_kernel, plan, slots, 0, True),
        (me, x, e, ge1, gx2, gk1, gv1, sq),
        (cube, cube, (2, *leaf_chunk), leaf_chunk, leaf_chunk),
        leaf_scratch,
    )
    grad_center, qkeep1, qgive1 = call(
        functools.partial(seventh_kernel, plan),
        (me, *gqs1, res1, h, sq),
        (cell, query_chunk, query_chunk),
        (ext, (wide, lanes), (graph_devices, *query_chunk[1:])),
    )

    def reduced(keep, give, q_keep, q_give, core, l_give, l_keep):
        return jnp.concatenate(
            [
                graph_scatter(keep, give, graph_devices),
                graph_scatter(q_keep, q_give, graph_devices),
                leaf_scatter(core, l_give, l_keep, sizes),
            ],
            axis=0,
        )

    chunks2 = reduced(keep2, give2, qkeep2, qgive2, lcore2, lgive2, lkeep2)
    chunks1 = reduced(keep1, give1, qkeep1, qgive1, lcore1, lgive1, lkeep1)
    pieces2, routes = gather(chunks2, sizes)
    pieces1, _ = gather(chunks1, sizes)
    g_square, g_out, g_in, g_down, g_hid, g_bias, g_gain = call(
        functools.partial(last_kernel, plan, routes),
        (me, *pieces1, *pieces2),
        ((LAYERS, width, 4, width), (width, LAYERS, width), (width, LAYERS, hidden), (width, LAYERS, hidden),
         (LAYERS, hidden), (7, LAYERS, width), (LAYERS, 2, width)),
        ((graph_devices, leaf_devices, plan.chunk_tiles * ROWS, LANES),),
    )
    return (
        center_out.T,
        e2.transpose(2, 1, 0),
        grad_center.T,
        gx1.transpose(2, 1, 0),
        ge0.transpose(2, 1, 0),
        g_square.transpose(0, 2, 1, 3),
        g_out.transpose(1, 0, 2),
        g_in.transpose(1, 0, 2),
        g_down.transpose(1, 2, 0),
        g_hid,
        g_bias.transpose(1, 0, 2),
        g_gain,
    )


def solution(mesh):
    sizes = (mesh.shape["graphs"], mesh.shape["leaves"])
    in_specs = (
        P("graphs", None),
        P("graphs", "leaves", None),
        P("graphs", "leaves", None),
        P("graphs"),
        P(),
        P(),
        P(),
        P(),
        P(),
        P(),
        P(),
        P("graphs", None),
        P("graphs", "leaves", None),
    )
    out_specs = (
        P("graphs", None),
        P("graphs", "leaves", None),
        P("graphs", None),
        P("graphs", "leaves", None),
        P("graphs", "leaves", None),
        P(),
        P(),
        P(),
        P(),
        P(),
        P(),
        P(),
    )
    return jax.shard_map(
        functools.partial(on_device, sizes),
        mesh=mesh,
        in_specs=in_specs,
        out_specs=out_specs,
        check_vma=False,
    )
```

time: 737 us -> 309 us (0.42)
  waiting for transfers between devices: 289 us -> 96.2 us
  blocking collectives: 128 us -> 0 us
  Pallas kernels: 0 us -> 123 us
  local copies, waits for them, and re-layouts: 125 us -> 4.74 us
  matrix products: 90.8 us -> 0 us
  starting transfers between devices: 0.25 us -> 76.2 us
  other arithmetic: 77.4 us -> 4.16 us
  between operations: 16.1 us -> 1.62 us
    psum x6 -> x0, waiting for transfers between devices: 289 us -> none  [the longest x1 140 us: on_device(): leaf_sum = lax.psum((leaf_stack[0], leaf_stack[1]), ('graphs', 'leaves'))]
    pallas_call x0 -> x9, Pallas kernels: none -> 123 us  [call(): pl.pallas_call(kernel, in_specs=[SMEM if first_smem and n == 0 else VMEM...]
    psum x4 -> x0, blocking collectives: 104 us -> none  [the longest x1 40.8 us: on_device(): leaf_sum = lax.psum((leaf_stack[0], leaf_stack[1]), ('graphs', 'leaves'))]
    ppermute x0 -> x74, waiting for transfers between devices: none -> 96.2 us  [swap(): return jax.tree.map(lambda v: lax.ppermute(v, axis, pairs), values)]
    dot_general x42 -> x0, matrix products: 90.8 us -> none  [matmul_hi(): return jnp.dot(left, right, precision=precise)]
    ppermute x0 -> x74, starting transfers between devices: none -> 76.2 us  [swap(): return jax.tree.map(lambda v: lax.ppermute(v, axis, pairs), values)]
    reshape x36 -> x0, local copies, waits for them, and re-layouts: 42.7 us -> none  [the longest x2 8.01 us: on_device(): jnp.einsum('ghs,ghc->gshc', probs, att_heads, precision=precise)]
    unnamed x253 -> x106, local copies, waits for them, and re-layouts: 30.6 us -> 4.64 us
  transfers between devices with their start and end apart: 6 -> 74, of which waited for: 5 -> 31; matrix products, arithmetic and copies ran while one was open for 22% -> 1% of each run, Pallas kernels for 0% -> 12%
where the time goes in v1:
time: 309 us; the launch traced here: 306 us
  Pallas kernels  123 us (40%)
  waiting for transfers between devices  96.2 us (31%)
  starting transfers between devices  76.2 us (25%)
  local copies, waits for them, and re-layouts  4.74 us (2%)
  other arithmetic  4.16 us (1%)
    pallas_call x9, Pallas kernels, call(): pl.pallas_call(kernel, in_specs=[SMEM if first_smem and n == 0 else VMEM...  123 us
    ppermute x74, waiting for transfers between devices, swap(): return jax.tree.map(lambda v: lax.ppermute(v, axis, pairs), values)  96.2 us
    ppermute x74, starting transfers between devices, swap(): return jax.tree.map(lambda v: lax.ppermute(v, axis, pairs), values)  76.2 us
  transfers between devices with their start and end apart: 74, of which 31 were waited for; matrix products, arithmetic and copies ran while one was open for 1% of the time, Pallas kernels for 12%

profile of v1, /device:TPU:0, one launch (start us, length us, event | category | flops | bytes accessed | tf_op | source)
XLA Modules:
  0.0 305.7 jit_solution(11453464156224165217)
XLA Ops:
  1.2 6.6 %shard_map.220 = (f32[336,128]{1,0:T(8,128)}, f32[300,128]{1,0:T(8,128)}, f32[300,512]{1,0:T(8,128)}, f32[300,512]{1,0:T(8,128)}, f32[4,16,128]{2,1,0:T(8,128)}, /*index=5*/f32[300,4,128]{2,1,0:T(4,128)}) custom-call(s32[2]{0:T(128)} %pad_add_fusion.me_ref, s32[1,128]{1,0:T(1,128)} %bitcast.128, f32[300,4,128]{2,1,0:T(4,128)} %bitcast.106, ...), custom_call_target="tpu_custom_call" | custom-call | tf_op jit(solution)/shard_map/pallas_call | solution.py:628
  10.9 6.2 %shard_map.221 = (f32[300,512]{1,0:T(8,128)}, f32[300,512]{1,0:T(8,128)}, f32[300,4,128]{2,1,0:T(4,128)}) custom-call(f32[300,4,128]{2,1,0:T(4,128)} %bitcast.107, f32[300,4,128]{2,1,0:T(4,128)} %get-tuple-element.69.e1_ref.e_ref, f32[2,300,4,300]{3,2,1,0:T(4,128)} %bitcast.94, f32[7,2,300]{2,1,0:T(2,128)} %bitcast.123), custom_call_target="tpu_custom_call" | custom-call | tf_op jit(solution)/shard_map/pallas_call | solution.py:628
  19.8 13.2 %shard_map.222 = (f32[336,128]{1,0:T(8,128)}, f32[300,128]{1,0:T(8,128)}, f32[16,128]{1,0:T(8,128)}, f32[16,128]{1,0:T(8,128)}, f32[300,128]{1,0:T(8,128)}, /*in...) custom-call(s32[2]{0:T(128)} %pad_add_fusion.me_ref, ...), custom_call_target="tpu_custom_call" | custom-call | tf_op jit(solution)/shard_map/pallas_call | solution.py:628
  35.5 4.7 %collective-permute-done.5.p3 = f32[336,128]{1,0:T(8,128)S(1)} collective-permute-done((f32[336,128]{1,0:T(8,128)}, f32[336,128]{1,0:T(8,128)S(1)}, u32[]{:S(2)}, u32[]{:S(2)}) %collective-permute-start.5) | collective-permute-done | bytes 172064 | tf_op jit(solution)/shard_map/ppermute | solution.py:519
  44.7 33.4 %shard_map.223 = (f32[300,128]{1,0:T(8,128)}, f32[300,128]{1,0:T(8,128)}, f32[300,512]{1,0:T(8,128)}, f32[300,512]{1,0:T(8,128)}, f32[300,128]{1,0:T(8,128)}, /*...) custom-call(s32[2]{0:T(128)} %pad_add_fusion.me_ref, f32[336,128]{1,0:T(8,128)} %get-tuple-element.72.p0, ...), custom_call_target="tpu_custom_call" | custom-call | tf_op jit(solution)/shard_map/pallas_call | solution.py:628
  80.3 4.1 %collective-permute-done.8.g3 = f32[300,128]{1,0:T(8,128)S(1)} collective-permute-done((f32[300,128]{1,0:T(8,128)}, f32[300,128]{1,0:T(8,128)S(1)}, u32[]{:S(2)}, u32[]{:S(2)}) %collective-permute-start.8) | collective-permute-done | bytes 153632 | tf_op jit(solution)/shard_map/ppermute | solution.py:519
  88.7 18.1 %shard_map.224 = (f32[300,128]{1,0:T(8,128)}, f32[300,512]{1,0:T(8,128)}, f32[300,512]{1,0:T(8,128)}, f32[300,128]{1,0:T(8,128)}, f32[4,224,128]{2,1,0:T(8,128)}...) custom-call(s32[2]{0:T(128)} %pad_add_fusion.me_ref, f32[300,128]{1,0:T(8,128)} %get-tuple-element.78.g0, ...), custom_call_target="tpu_custom_call" | custom-call | tf_op jit(solution)/shard_map/pallas_call | solution.py:628
  112.3 4.1 %collective-permute-start.50 = (f32[1,32,128]{2,1,0:T(8,128)S(1)}, f32[1,32,128]{2,1,0:T(8,128)S(1)}, u32[]{:S(2)}, u32[]{:S(2)}) collective-permute-start(f32[1,32,128]{2,1,0:T(8,128)S(1)} %get-tuple-element.152), channel_id=1, source_target_pairs={{0,24},{4,28},{8,16},{12,20},{16,8},{20,12},{24,0},{28,4},{1,25},{... | collective-permute-start | bytes 49160 | tf_op jit(solution)/shard_map/ppermute | solution.py:519
  119.0 12.9 %shard_map.226 = (f32[300,4,128]{2,1,0:T(4,128)}, f32[300,4,128]{2,1,0:T(4,128)}, f32[2,8,80,128]{3,2,1,0:T(8,128)}, f32[8,80,128]{2,1,0:T(8,128)}, f32[8,80,128]{2,1,0:T(8,128)}) custom-call(s32[2]{0:T(128)} %pad_add_fusion.me_ref, f32[300,4,128]{2,1,0:T(4,128)} %bitcast.108, f32[300,4,128]{2,1,0:T(4,128)} %get-tuple-element.69.e1_ref.e_ref, ...), custom_call_target="tpu_custom_call" | custom-call | tf_op jit(solution)/shard_map/pallas_call | solution.py:628
  131.8 13.5 %shard_map.227 = (f32[300,4,128]{2,1,0:T(4,128)}, f32[300,4,128]{2,1,0:T(4,128)}, f32[2,8,80,128]{3,2,1,0:T(8,128)}, f32[8,80,128]{2,1,0:T(8,128)}, f32[8,80,128]{2,1,0:T(8,128)}) custom-call(s32[2]{0:T(128)} %pad_add_fusion.me_ref, f32[300,4,128]{2,1,0:T(4,128)} %bitcast.109, f32[300,4,128]{2,1,0:T(4,128)} %bitcast.118, ...), custom_call_target="tpu_custom_call" | custom-call | tf_op jit(solution)/shard_map/pallas_call | solution.py:628
  146.1 4.8 %shard_map.225 = (f32[300,128]{1,0:T(8,128)}, f32[4,32,128]{2,1,0:T(8,128)}, f32[4,32,128]{2,1,0:T(8,128)}) custom-call(s32[2]{0:T(128)} %pad_add_fusion.me_ref, f32[300,128]{1,0:T(8,128)} %get-tuple-element.92.g0, f32[300,128]{1,0:T(8,128)} %copy-done.48, f32[300,128]{1,0:T(8,128)} %copy-done.47, f32[300,128]{1,0:T(8,128)} %copy-done.46, ...), custom_call_target="tpu_custom_call" | custom-call | tf_op jit(solution)/shard_map/pallas_call | solution.py:628
  153.7 11.2 %collective-permute-done.16 = f32[4,32,128]{2,1,0:T(8,128)S(1)} collective-permute-done((f32[4,32,128]{2,1,0:T(8,128)}, f32[4,32,128]{2,1,0:T(8,128)S(1)}, u32[]{:S(2)}, u32[]{:S(2)}) %collective-permute-start.16) | collective-permute-done | bytes 65568 | tf_op jit(solution)/shard_map/ppermute | solution.py:519
  165.7 3.9 %collective-permute-start.19 = (f32[1,32,128]{2,1,0:T(8,128)S(1)}, f32[1,32,128]{2,1,0:T(8,128)S(1)}, u32[]{:S(2)}, u32[]{:S(2)}) collective-permute-start(f32[1,32,128]{2,1,0:T(8,128)S(1)} %get-tuple-element.155), channel_id=1, source_target_pairs={{0,24},{4,28},{8,16},{12,20},{16,8},{20,12},{24,0},{28,4},{1,25},{... | collective-permute-start | bytes 49160 | tf_op jit(solution)/shard_map/ppermute | solution.py:519
  171.3 3.9 %collective-permute-start.46 = (f32[1,224,128]{2,1,0:T(8,128)S(1)}, f32[1,224,128]{2,1,0:T(8,128)S(1)}, u32[]{:S(2)}, u32[]{:S(2)}) collective-permute-start(f32[1,224,128]{2,1,0:T(8,128)S(1)} %get-tuple-element.128), channel_id=1, source_target_pairs={{0,24},{4,28},{8,16},{12,20},{16,8},{20,12},{24,0},{28,4},{1,25},{... | collective-permute-start | bytes 344072 | tf_op jit(solution)/shard_map/ppermute | solution.py:519
  178.4 4.3 %collective-permute-done.45 = f32[1,224,128]{2,1,0:T(8,128)S(1)} collective-permute-done((f32[1,224,128]{2,1,0:T(8,128)S(1)}, f32[1,224,128]{2,1,0:T(8,128)S(1)}, u32[]{:S(2)}, u32[]{:S(2)}) %collective-permute-start.45) | collective-permute-done | bytes 114720 | tf_op jit(solution)/shard_map/ppermute | solution.py:519
  189.6 3.9 %collective-permute-done.52 = f32[8,80,128]{2,1,0:T(8,128)S(1)} collective-permute-done((f32[8,80,128]{2,1,0:T(8,128)S(1)}, f32[8,80,128]{2,1,0:T(8,128)S(1)}, u32[]{:S(2)}, u32[]{:S(2)}) %collective-permute-start.52) | collective-permute-done | bytes 327712 | tf_op jit(solution)/shard_map/ppermute | solution.py:519
  222.6 6.8 %collective-permute-start.26 = (f32[336,128]{1,0:T(8,128)S(1)}, f32[336,128]{1,0:T(8,128)S(1)}, u32[]{:S(2)}, u32[]{:S(2)}) collective-permute-start(f32[336,128]{1,0:T(8,128)S(1)} %pad_maximum_fusion.4), channel_id=1, source_target_pairs={{0,8},{4,12},{8,0},{12,4},{16,24},{20,28},{24,16},{28,20},{1,9},{5... | collective-permute-start | bytes 516104 | tf_op jit(solution)/shard_map/ppermute | solution.py:519
  229.4 6.8 %collective-permute-done.58 = f32[336,128]{1,0:T(8,128)S(1)} collective-permute-done((f32[336,128]{1,0:T(8,128)S(1)}, f32[336,128]{1,0:T(8,128)S(1)}, u32[]{:S(2)}, u32[]{:S(2)}) %collective-permute-start.58) | collective-permute-done | bytes 172064 | tf_op jit(solution)/shard_map/ppermute | solution.py:519
  243.3 4.0 %collective-permute-done.61.refs_18_ = f32[4,168,128]{2,1,0:T(8,128)S(1)} collective-permute-done((f32[4,168,128]{2,1,0:T(8,128)S(1)}, f32[4,168,128]{2,1,0:T(8,128)S(1)}, u32[]{:S(2)}, u32[]{:S(2)}) %collective-permute-start.61) | collective-permute-done | bytes 344096 | tf_op jit(solution)/shard_map/ppermute | solution.py:519
  251.3 4.2 %collective-permute-done.68.refs_26_ = f32[4,168,128]{2,1,0:T(8,128)S(1)} collective-permute-done((f32[4,168,128]{2,1,0:T(8,128)S(1)}, f32[4,168,128]{2,1,0:T(8,128)S(1)}, u32[]{:S(2)}, u32[]{:S(2)}) %collective-permute-start.68) | collective-permute-done | bytes 344096 | tf_op jit(solution)/shard_map/ppermute | solution.py:519
  264.3 5.2 %collective-permute-done.37.refs_10_ = f32[4,168,128]{2,1,0:T(8,128)S(1)} collective-permute-done((f32[4,168,128]{2,1,0:T(8,128)S(1)}, f32[4,168,128]{2,1,0:T(8,128)S(1)}, u32[]{:S(2)}, u32[]{:S(2)}) %collective-permute-start.37) | collective-permute-done | bytes 344096 | tf_op jit(solution)/shard_map/ppermute | solution.py:519
  271.6 4.8 %collective-permute-done.62.refs_19_ = f32[4,168,128]{2,1,0:T(8,128)S(1)} collective-permute-done((f32[4,168,128]{2,1,0:T(8,128)S(1)}, f32[4,168,128]{2,1,0:T(8,128)S(1)}, u32[]{:S(2)}, u32[]{:S(2)}) %collective-permute-start.62) | collective-permute-done | bytes 344096 | tf_op jit(solution)/shard_map/ppermute | solution.py:519
  282.2 4.7 %collective-permute-done.31.refs_3_ = f32[4,168,128]{2,1,0:T(8,128)S(1)} collective-permute-done((f32[4,168,128]{2,1,0:T(8,128)S(1)}, f32[4,168,128]{2,1,0:T(8,128)S(1)}, u32[]{:S(2)}, u32[]{:S(2)}) %collective-permute-start.31) | collective-permute-done | bytes 344096 | tf_op jit(solution)/shard_map/ppermute | solution.py:519
  291.4 14.1 %shard_map.228 = (f32[2,300,4,300]{3,2,1,0:T(4,128)}, f32[300,2,300]{2,1,0:T(2,128)}, f32[300,2,1200]{2,1,0:T(2,128)}, f32[300,2,1200]{2,1,0:T(2,128)}, f32[2,12...) custom-call(s32[2]{0:T(128)} %pad_add_fusion.me_ref, f32[4,168,128]{2,1,0:T(8,128)} %copy-done.2, ...), custom_call_target="tpu_custom_call" | custom-call | tf_op jit(solution)/shard_map/pallas_call | solution.py:628
  (272 shorter events, 104.9 us)
Async XLA Ops:
  110.5 34.9 %collective-permute-start.9 = (f32[300,128]{1,0:T(8,128)}, f32[300,128]{1,0:T(8,128)S(1)}, u32[]{:S(2)}, u32[]{:S(2)}) collective-permute-start(f32[300,128]{1,0:T(8,128)} %get-tuple-element.92.g0), channel_id=1, source_target_pairs={{0,1},{1,0},{2,3},{3,2},{4,5},{5,4},{6,7},{7,6},{8,9},{9,8},{10,11... | collective-permute-start | bytes 460808 | tf_op jit(solution)/shard_map/ppermute | solution.py:519
  112.3 38.6 %collective-permute-start.50 = (f32[1,32,128]{2,1,0:T(8,128)S(1)}, f32[1,32,128]{2,1,0:T(8,128)S(1)}, u32[]{:S(2)}, u32[]{:S(2)}) collective-permute-start(f32[1,32,128]{2,1,0:T(8,128)S(1)} %get-tuple-element.152), channel_id=1, source_target_pairs={{0,24},{4,28},{8,16},{12,20},{16,8},{20,12},{24,0},{28,4},{1,25},{... | collective-permute-start | bytes 49160 | tf_op jit(solution)/shard_map/ppermute | solution.py:519
  116.4 36.5 %collective-permute-start.49 = (f32[1,32,128]{2,1,0:T(8,128)S(1)}, f32[1,32,128]{2,1,0:T(8,128)S(1)}, u32[]{:S(2)}, u32[]{:S(2)}) collective-permute-start(f32[1,32,128]{2,1,0:T(8,128)S(1)} %get-tuple-element.153), channel_id=1, source_target_pairs={{0,16},{4,20},{8,24},{12,28},{16,0},{20,4},{24,8},{28,12},{1,17},{... | collective-permute-start | bytes 49160 | tf_op jit(solution)/shard_map/ppermute | solution.py:519
  116.4 36.6 %collective-permute-start.48 = (f32[1,32,128]{2,1,0:T(8,128)S(1)}, f32[1,32,128]{2,1,0:T(8,128)S(1)}, u32[]{:S(2)}, u32[]{:S(2)}) collective-permute-start(f32[1,32,128]{2,1,0:T(8,128)S(1)} %get-tuple-element.154), channel_id=1, source_target_pairs={{0,8},{4,12},{8,0},{12,4},{16,24},{20,28},{24,16},{28,20},{1,9},{5... | collective-permute-start | bytes 49160 | tf_op jit(solution)/shard_map/ppermute | solution.py:519
  118.9 50.7 %collective-permute-start.43 = (f32[4,224,128]{2,1,0:T(8,128)S(1)}, f32[4,224,128]{2,1,0:T(8,128)S(1)}, u32[]{:S(2)}, u32[]{:S(2)}) collective-permute-start(f32[4,224,128]{2,1,0:T(8,128)S(1)} %copy-done.52), channel_id=1, source_target_pairs={{0,4},{4,0},{8,12},{12,8},{16,20},{20,16},{24,28},{28,24},{1,5},{5... | collective-permute-start | bytes 1376264 | tf_op jit(solution)/shard_map/ppermute | solution.py:519
  145.4 37.4 %collective-permute-start.51 = (f32[2,8,80,128]{3,2,1,0:T(8,128)S(1)}, f32[2,8,80,128]{3,2,1,0:T(8,128)S(1)}, u32[]{:S(2)}, u32[]{:S(2)}) collective-permute-start(f32[2,8,80,128]{3,2,1,0:T(8,128)S(1)} %copy-done.50), channel_id=1, source_target_pairs={{0,1},{1,0},{2,3},{3,2},{4,5},{5,4},{6,7},{7,6},{8,9},{9,8},{10,11... | collective-permute-start | bytes 1966088 | tf_op jit(solution)/shard_map/ppermute | solution.py:519
  150.9 33.6 %collective-permute-start.12 = (f32[4,224,128]{2,1,0:T(8,128)S(1)}, f32[4,224,128]{2,1,0:T(8,128)S(1)}, u32[]{:S(2)}, u32[]{:S(2)}) collective-permute-start(f32[4,224,128]{2,1,0:T(8,128)S(1)} %copy-done.51), channel_id=1, source_target_pairs={{0,4},{4,0},{8,12},{12,8},{16,20},{20,16},{24,28},{28,24},{1,5},{5... | collective-permute-start | bytes 1376264 | tf_op jit(solution)/shard_map/ppermute | solution.py:519
  152.9 12.0 %collective-permute-start.16 = (f32[4,32,128]{2,1,0:T(8,128)}, f32[4,32,128]{2,1,0:T(8,128)S(1)}, u32[]{:S(2)}, u32[]{:S(2)}) collective-permute-start(f32[4,32,128]{2,1,0:T(8,128)} %get-tuple-element.106), channel_id=1, source_target_pairs={{0,4},{4,0},{8,12},{12,8},{16,20},{20,16},{24,28},{28,24},{1,5},{5... | collective-permute-start | bytes 196616 | tf_op jit(solution)/shard_map/ppermute | solution.py:519
  184.5 10.6 %collective-permute-start.15 = (f32[1,224,128]{2,1,0:T(8,128)S(1)}, f32[1,224,128]{2,1,0:T(8,128)S(1)}, u32[]{:S(2)}, u32[]{:S(2)}) collective-permute-start(f32[1,224,128]{2,1,0:T(8,128)S(1)} %get-tuple-element.131), channel_id=1, source_target_pairs={{0,24},{4,28},{8,16},{12,20},{16,8},{20,12},{24,0},{28,4},{1,25},{... | collective-permute-start | bytes 344072 | tf_op jit(solution)/shard_map/ppermute | solution.py:519
  189.0 14.4 %collective-permute-start.21 = (f32[8,80,128]{2,1,0:T(8,128)S(1)}, f32[8,80,128]{2,1,0:T(8,128)S(1)}, u32[]{:S(2)}, u32[]{:S(2)}) collective-permute-start(f32[8,80,128]{2,1,0:T(8,128)S(1)} %fusion.1), channel_id=1, source_target_pairs={{0,2},{1,3},{2,0},{3,1},{4,6},{5,7},{6,4},{7,5},{8,10},{9,11},{10,... | collective-permute-start | bytes 983048 | tf_op jit(solution)/shard_map/ppermute | solution.py:519
  214.8 21.4 %collective-permute-start.58 = (f32[336,128]{1,0:T(8,128)S(1)}, f32[336,128]{1,0:T(8,128)S(1)}, u32[]{:S(2)}, u32[]{:S(2)}) collective-permute-start(f32[336,128]{1,0:T(8,128)S(1)} %pad_maximum_fusion.5), channel_id=1, source_target_pairs={{0,16},{4,20},{8,24},{12,28},{16,0},{20,4},{24,8},{28,12},{1,17},{... | collective-permute-start | bytes 516104 | tf_op jit(solution)/shard_map/ppermute | solution.py:519
  215.3 20.9 %collective-permute-start.57 = (f32[336,128]{1,0:T(8,128)S(1)}, f32[336,128]{1,0:T(8,128)S(1)}, u32[]{:S(2)}, u32[]{:S(2)}) collective-permute-start(f32[336,128]{1,0:T(8,128)S(1)} %pad_maximum_fusion.5), channel_id=1, source_target_pairs={{0,8},{4,12},{8,0},{12,4},{16,24},{20,28},{24,16},{28,20},{1,9},{5... | collective-permute-start | bytes 516104 | tf_op jit(solution)/shard_map/ppermute | solution.py:519
  217.8 19.4 %collective-permute-start.28 = (f32[336,128]{1,0:T(8,128)S(1)}, f32[336,128]{1,0:T(8,128)S(1)}, u32[]{:S(2)}, u32[]{:S(2)}) collective-permute-start(f32[336,128]{1,0:T(8,128)S(1)} %pad_maximum_fusion.4), channel_id=1, source_target_pairs={{0,24},{4,28},{8,16},{12,20},{16,8},{20,12},{24,0},{28,4},{1,25},{... | collective-permute-start | bytes 516104 | tf_op jit(solution)/shard_map/ppermute | solution.py:519
  220.1 21.2 %collective-permute-start.27 = (f32[336,128]{1,0:T(8,128)S(1)}, f32[336,128]{1,0:T(8,128)S(1)}, u32[]{:S(2)}, u32[]{:S(2)}) collective-permute-start(f32[336,128]{1,0:T(8,128)S(1)} %pad_maximum_fusion.4), channel_id=1, source_target_pairs={{0,16},{4,20},{8,24},{12,28},{16,0},{20,4},{24,8},{28,12},{1,17},{... | collective-permute-start | bytes 516104 | tf_op jit(solution)/shard_map/ppermute | solution.py:519
  222.6 18.8 %collective-permute-start.26 = (f32[336,128]{1,0:T(8,128)S(1)}, f32[336,128]{1,0:T(8,128)S(1)}, u32[]{:S(2)}, u32[]{:S(2)}) collective-permute-start(f32[336,128]{1,0:T(8,128)S(1)} %pad_maximum_fusion.4), channel_id=1, source_target_pairs={{0,8},{4,12},{8,0},{12,4},{16,24},{20,28},{24,16},{28,20},{1,9},{5... | collective-permute-start | bytes 516104 | tf_op jit(solution)/shard_map/ppermute | solution.py:519
  236.4 10.9 %collective-permute-start.61 = (f32[4,168,128]{2,1,0:T(8,128)S(1)}, f32[4,168,128]{2,1,0:T(8,128)S(1)}, u32[]{:S(2)}, u32[]{:S(2)}) collective-permute-start(f32[4,168,128]{2,1,0:T(8,128)S(1)} %pad_maximum_fusion.2.refs_16_), channel_id=1, source_target_pairs={{0,2},{1,3},{2,0},{3,1},{4,6},{5,7},{6,4},{7,5},{8,10},{9,11},{10,... | collective-permute-start | bytes 1032200 | tf_op jit(solution)/shard_map/ppermute | solution.py:519
  237.2 11.0 %collective-permute-start.60 = (f32[4,168,128]{2,1,0:T(8,128)S(1)}, f32[4,168,128]{2,1,0:T(8,128)S(1)}, u32[]{:S(2)}, u32[]{:S(2)}) collective-permute-start(f32[4,168,128]{2,1,0:T(8,128)S(1)} %pad_maximum_fusion.2.refs_16_), channel_id=1, source_target_pairs={{0,4},{4,0},{8,12},{12,8},{16,20},{20,16},{24,28},{28,24},{1,5},{5... | collective-permute-start | bytes 1032200 | tf_op jit(solution)/shard_map/ppermute | solution.py:519
  241.4 14.2 %collective-permute-start.68 = (f32[4,168,128]{2,1,0:T(8,128)S(1)}, f32[4,168,128]{2,1,0:T(8,128)S(1)}, u32[]{:S(2)}, u32[]{:S(2)}) collective-permute-start(f32[4,168,128]{2,1,0:T(8,128)S(1)} %pad_maximum_fusion.3.refs_24_), channel_id=1, source_target_pairs={{0,4},{4,0},{8,12},{12,8},{16,20},{20,16},{24,28},{28,24},{1,5},{5... | collective-permute-start | bytes 1032200 | tf_op jit(solution)/shard_map/ppermute | solution.py:519
  243.0 12.5 %collective-permute-start.67 = (f32[4,168,128]{2,1,0:T(8,128)S(1)}, f32[4,168,128]{2,1,0:T(8,128)S(1)}, u32[]{:S(2)}, u32[]{:S(2)}) collective-permute-start(f32[4,168,128]{2,1,0:T(8,128)S(1)} %pad_maximum_fusion.3.refs_24_), channel_id=1, source_target_pairs={{0,2},{1,3},{2,0},{3,1},{4,6},{5,7},{6,4},{7,5},{8,10},{9,11},{10,... | collective-permute-start | bytes 1032200 | tf_op jit(solution)/shard_map/ppermute | solution.py:519
  248.2 13.9 %collective-permute-start.30 = (f32[4,168,128]{2,1,0:T(8,128)S(1)}, f32[4,168,128]{2,1,0:T(8,128)S(1)}, u32[]{:S(2)}, u32[]{:S(2)}) collective-permute-start(f32[4,168,128]{2,1,0:T(8,128)S(1)} %pad_maximum_fusion.refs_0_), channel_id=1, source_target_pairs={{0,2},{1,3},{2,0},{3,1},{4,6},{5,7},{6,4},{7,5},{8,10},{9,11},{10,... | collective-permute-start | bytes 1032200 | tf_op jit(solution)/shard_map/ppermute | solution.py:519
  249.6 13.4 %collective-permute-start.29 = (f32[4,168,128]{2,1,0:T(8,128)S(1)}, f32[4,168,128]{2,1,0:T(8,128)S(1)}, u32[]{:S(2)}, u32[]{:S(2)}) collective-permute-start(f32[4,168,128]{2,1,0:T(8,128)S(1)} %pad_maximum_fusion.refs_0_), channel_id=1, source_target_pairs={{0,4},{4,0},{8,12},{12,8},{16,20},{20,16},{24,28},{28,24},{1,5},{5... | collective-permute-start | bytes 1032200 | tf_op jit(solution)/shard_map/ppermute | solution.py:519
  255.6 14.0 %collective-permute-start.37 = (f32[4,168,128]{2,1,0:T(8,128)S(1)}, f32[4,168,128]{2,1,0:T(8,128)S(1)}, u32[]{:S(2)}, u32[]{:S(2)}) collective-permute-start(f32[4,168,128]{2,1,0:T(8,128)S(1)} %pad_maximum_fusion.1.refs_8_), channel_id=1, source_target_pairs={{0,4},{4,0},{8,12},{12,8},{16,20},{20,16},{24,28},{28,24},{1,5},{5... | collective-permute-start | bytes 1032200 | tf_op jit(solution)/shard_map/ppermute | solution.py:519
  257.2 12.4 %collective-permute-start.36 = (f32[4,168,128]{2,1,0:T(8,128)S(1)}, f32[4,168,128]{2,1,0:T(8,128)S(1)}, u32[]{:S(2)}, u32[]{:S(2)}) collective-permute-start(f32[4,168,128]{2,1,0:T(8,128)S(1)} %pad_maximum_fusion.1.refs_8_), channel_id=1, source_target_pairs={{0,2},{1,3},{2,0},{3,1},{4,6},{5,7},{6,4},{7,5},{8,10},{9,11},{10,... | collective-permute-start | bytes 1032200 | tf_op jit(solution)/shard_map/ppermute | solution.py:519
  262.9 13.4 %collective-permute-start.62 = (f32[4,168,128]{2,1,0:T(8,128)S(1)}, f32[4,168,128]{2,1,0:T(8,128)S(1)}, u32[]{:S(2)}, u32[]{:S(2)}) collective-permute-start(f32[4,168,128]{2,1,0:T(8,128)S(1)} %collective-permute-done.60.refs_17_), channel_id=1, source_target_pairs={{0,2},{1,3},{2,0},{3,1},{4,6},{5,7},{6,4},{7,5},{8,10},{9,11},{10,... | collective-permute-start | bytes 1032200 | tf_op jit(solution)/shard_map/ppermute | solution.py:519
  (103 other events, 1437.2 us)
